TPU v7x, 32 devices: a whole 2x2x4 slice. The times are simulated.
32 devices in a mesh: px: 4 (over z), py: 8 (over y, x, core).
Axes of the slice: x: 2, y: 2, z: 4, core: 2. Of those that a mesh axis runs over, the one named last changes fastest.
Arguments:
- fractions: float32 [1024, 3, 128], P(('px', 'py')), may hold values from 0 to 1
- charge: float32 [1024, 128], P(('px', 'py')), may hold values from -4 to 4
- cell_index: int32 [1024, 128], P(('px', 'py')), may hold values from 0 to 524287
- destination: int32 [1024, 1], P(('px', 'py')), may hold values from 0 to 7; in each aligned block of 32 rows (0 to 31, 32 to 63, ...) at most 6 rows name the same one
- live_blocks: int32 [32], P(('px', 'py')), may hold values from 16 to 32, as said below
Outputs:
- forces: float32 [1024, 3, 128], P(('px', 'py'))
Inputs may be any that keep to these rules, and one draw needn't show every extreme that they name: `destination`: in the rows of one device no value is named by more than 6 blocks, a bound that some block reaches. `live_blocks`: some domain has all 32 slots occupied in every draw.
All inputs are finite; a program needn't handle non-finite values.
Results may differ from a plain program's by a relative error of at most 0.0003.
Values sent between devices are 32-bit elements; how exact they have to be, the bound alone decides.
A program may use at most 128 MiB of HBM per device.

v0:
```python
import math

import jax
import jax.numpy as jnp
import numpy as np
from jax import lax
from jax.experimental import pallas as pl
from jax.experimental.pallas import tpu as pltpu
from jax.sharding import PartitionSpec as P

K = 256
EWALD_GAIN = 4.0
EWALD_BETA = 0.6
SPLINE_SUMS = (1.0 / 120.0, 26.0 / 120.0, 66.0 / 120.0, 26.0 / 120.0, 1.0 / 120.0)
HIGHEST = lax.Precision.HIGHEST
HIGH = lax.Precision.HIGH
LANES = 128
ROWS_CHUNK = 10
SORT_BLOCKS = 8
GROUP_BLOCKS = 2


def hartley():
    steps = np.arange(K)
    angle = 2.0 * math.pi / K * (np.outer(steps, steps) % K)
    return (np.cos(angle) + np.sin(angle)).astype(np.float32)


def wave_profile():
    steps = np.arange(K)
    folded = np.where(2 * steps < K, steps, steps - K) / K
    waves = np.exp(2j * math.pi / K * np.outer(steps, np.arange(5)))
    modulus = 1.0 / np.abs(waves @ np.array(SPLINE_SUMS)) ** 2
    squared = folded * folded
    gauss = np.exp(-(math.pi * math.pi) * squared / (EWALD_BETA * EWALD_BETA))
    return squared.astype(np.float32), (gauss * modulus).astype(np.float32)


def from_behind(value, axis, steps):
    count = lax.axis_size(axis)
    pairs = [(source, (source + steps) % count) for source in range(count)]
    return lax.ppermute(value, axis, pairs)


def spline_six(u):
    older_values = [1.0 - u, u]
    slopes = []
    for spline_order in range(3, 7):
        newer_values = []
        for k in range(spline_order):
            terms = []
            if k >= 1:
                terms.append((u + (spline_order - 1 - k)) * older_values[k - 1])
            if k <= spline_order - 2:
                terms.append((k + 1 - u) * older_values[k])
            newer_values.append(sum(terms[1:], terms[0]) * (1.0 / (spline_order - 1)))
        if spline_order == 6:
            slopes = [-older_values[0]]
            slopes += [older_values[k - 1] - older_values[k] for k in range(1, 5)]
            slopes += [older_values[4]]
        older_values = newer_values
    return (older_values, slopes)


def placed(offset, values):
    table = jnp.zeros(offset.shape, jnp.float32)
    for k in range(6):
        table = jnp.where(offset == k, values[k], table)
    return table


def offsets(base, rows, wrap):
    width = base.shape[1]
    offset = lax.broadcasted_iota(jnp.int32, (rows, width), 0) - base
    return offset & (K - 1) if wrap else offset


def halves(value):
    upper = value.astype(jnp.bfloat16)
    lower = (value - upper.astype(jnp.float32)).astype(jnp.bfloat16)
    return upper, lower


def touched(span_ref, step, start):
    return (span_ref[0, step] < start + ROWS_CHUNK) & (span_ref[1, step] + 5 >= start)


def deposit_kernel(span_ref, atoms_ref, grid_ref):
    step = pl.program_id(0)
    rows, columns, depth = grid_ref.shape
    width = atoms_ref.shape[2]

    @pl.when(step == 0)
    def _():
        grid_ref[...] = jnp.zeros(grid_ref.shape, jnp.float32)

    @pl.when(span_ref[1, step] >= 0)
    def _():
        atoms = atoms_ref[0]
        base = atoms.astype(jnp.int32)
        table_x = placed(offsets(base[4:5], rows, False), spline_six(atoms[0:1])[0])
        table_y = placed(offsets(base[5:6], columns, False), spline_six(atoms[1:2])[0])
        table_z = placed(offsets(base[6:7], depth, True), spline_six(atoms[2:3])[0])
        upper, lower = halves((table_z * atoms[3:4]).T)
        weights = jnp.concatenate([upper, lower, upper], axis=0)
        for start in range(0, rows, ROWS_CHUNK):

            @pl.when(touched(span_ref, step, start))
            def _(start=start):
                chunk = table_x[start : start + ROWS_CHUNK]
                outer = (chunk[:, None, :] * table_y[None, :, :]).reshape(-1, width)
                upper, lower = halves(outer)
                spread = jnp.dot(
                    jnp.concatenate([upper, upper, lower], axis=1),
                    weights,
                    preferred_element_type=jnp.float32,
                )
                grid_ref[start : start + ROWS_CHUNK] += spread.reshape(-1, columns, depth)


def pull_kernel(span_ref, atoms_ref, potential_ref, forces_ref, parts, totals):
    step = pl.program_id(0)
    rows, columns, depth = potential_ref.shape
    width = atoms_ref.shape[2]
    piece = ROWS_CHUNK * columns

    @pl.when(step == 0)
    def _():
        for index in range(rows // ROWS_CHUNK):
            start = index * ROWS_CHUNK
            values = potential_ref[start : start + ROWS_CHUNK].reshape(piece, depth)
            upper, lower = halves(values)
            parts[index * piece : (index + 1) * piece] = jnp.concatenate(
                [upper, lower, upper], axis=1
            )

    @pl.when(span_ref[1, step] < 0)
    def _():
        forces_ref[...] = jnp.zeros(forces_ref.shape, jnp.float32)

    @pl.when(span_ref[1, step] >= 0)
    def _():
        atoms = atoms_ref[0]
        base = atoms.astype(jnp.int32)
        offset_x = offsets(base[4:5], rows, False)
        offset_y = offsets(base[5:6], columns, False)
        offset_z = offsets(base[6:7], depth, True)
        values, slopes = spline_six(atoms[0:1])
        table_x, slope_x = placed(offset_x, values), placed(offset_x, slopes)
        values, slopes = spline_six(atoms[1:2])
        table_y, slope_y = placed(offset_y, values), placed(offset_y, slopes)
        values, slopes = spline_six(atoms[2:3])
        both = jnp.concatenate([placed(offset_z, values), placed(offset_z, slopes)], axis=1)
        upper, lower = halves(both)
        weights = jnp.concatenate([upper, upper, lower], axis=0)
        totals[...] = jnp.zeros(totals.shape, jnp.float32)

        def folded(terms):
            return jnp.sum(terms.reshape(columns // 8, 8, width), axis=0)

        for index in range(rows // ROWS_CHUNK):

            @pl.when(touched(span_ref, step, index * ROWS_CHUNK))
            def _(index=index):
                start = index * ROWS_CHUNK
                sampled = jnp.dot(
                    parts[index * piece : (index + 1) * piece],
                    weights,
                    preferred_element_type=jnp.float32,
                ).reshape(ROWS_CHUNK, columns, 2 * width)
                sums = [totals[0], totals[1], totals[2]]
                for row in range(ROWS_CHUNK):
                    plain = sampled[row, :, :width]
                    sloped = sampled[row, :, width:]
                    value_x = table_x[start + row : start + row + 1]
                    turned_x = slope_x[start + row : start + row + 1]
                    sums[0] = sums[0] + turned_x * folded(plain * table_y)
                    sums[1] = sums[1] + value_x * folded(plain * slope_y)
                    sums[2] = sums[2] + value_x * folded(sloped * table_y)
                for axis in range(3):
                    totals[axis] = sums[axis]

        result = [-atoms[3:4] * jnp.sum(totals[axis], axis=0, keepdims=True) for axis in range(3)]
        forces_ref[0] = jnp.concatenate(
            result + [jnp.zeros((5, width), jnp.float32)], axis=0
        )


def deposit(count, atoms, rows, columns):
    groups, lines, width = atoms.shape
    return pl.pallas_call(
        deposit_kernel,
        out_shape=jax.ShapeDtypeStruct((rows, columns, K), jnp.float32),
        grid=(groups,),
        in_specs=[
            pl.BlockSpec(memory_space=pltpu.SMEM),
            pl.BlockSpec((1, lines, width), lambda g: (g, 0, 0)),
        ],
        out_specs=pl.BlockSpec((rows, columns, K), lambda g: (0, 0, 0)),
        compiler_params=pltpu.CompilerParams(vmem_limit_bytes=48 * 2**20),
        name="deposit",
    )(count, atoms)


def pull(count, atoms, potential):
    groups, lines, width = atoms.shape
    rows, columns, _ = potential.shape
    return pl.pallas_call(
        pull_kernel,
        out_shape=jax.ShapeDtypeStruct((groups, lines, width), jnp.float32),
        grid=(groups,),
        in_specs=[
            pl.BlockSpec(memory_space=pltpu.SMEM),
            pl.BlockSpec((1, lines, width), lambda g: (g, 0, 0)),
            pl.BlockSpec((rows, columns, K), lambda g: (0, 0, 0)),
        ],
        out_specs=pl.BlockSpec((1, lines, width), lambda g: (g, 0, 0)),
        scratch_shapes=[
            pltpu.VMEM((rows * columns, 3 * K), jnp.bfloat16),
            pltpu.VMEM((3, 8, width), jnp.float32),
        ],
        compiler_params=pltpu.CompilerParams(vmem_limit_bytes=48 * 2**20),
        name="pull",
    )(count, atoms, potential)


def exact_halves(values):
    upper = values.astype(jnp.bfloat16)
    return upper, (values - upper.astype(np.float32)).astype(jnp.bfloat16)


def product(left, right, transposed=False):
    dims = (((1,), (1 if transposed else 0,)), ((), ()))

    def one(a, b):
        return lax.dot_general(a, b, dims, preferred_element_type=jnp.float32)

    return one(left[0], right[0]) + (one(left[1], right[0]) + one(left[0], right[1]))


def convolve_kernel(
    counts,
    spectrum_ref,
    gain_ref,
    mix_upper,
    mix_lower,
    wave_upper,
    wave_lower,
    out_ref,
    columns_in,
    rows_out,
    rows_in,
    back_out,
    back_in,
    columns_out,
    send_sems,
    recv_sems,
    local_sems,
):
    chunks, step, bands = counts
    rows_dev = lax.axis_size("px")
    cols_dev = lax.axis_size("py")
    index_x = lax.axis_index("px")
    index_y = lax.axis_index("py")
    lines = step * bands
    packed = mix_upper.shape[1] // K
    span_x = packed * bands

    barrier = pltpu.get_barrier_semaphore()
    for axis, count, index in (("px", rows_dev, index_x), ("py", cols_dev, index_y)):
        for shift in range(1, count):
            pl.semaphore_signal(
                barrier,
                inc=1,
                device_id={axis: lax.rem(index + shift, count)},
                device_id_type=pl.DeviceIdType.MESH,
            )
    pl.semaphore_wait(barrier, rows_dev + cols_dev - 2)

    def exchange(stage, chunk, axis, source, target):
        count, index = (rows_dev, index_x) if axis == "px" else (cols_dev, index_y)
        copies = []
        for shift in range(1, count):
            peer = lax.rem(index + shift, count)
            copies.append(
                pltpu.make_async_remote_copy(
                    src_ref=source(peer),
                    dst_ref=target(index),
                    send_sem=send_sems.at[stage, chunk, shift],
                    recv_sem=recv_sems.at[stage, chunk, shift],
                    device_id={axis: peer},
                    device_id_type=pl.DeviceIdType.MESH,
                )
            )
        copies.append(
            pltpu.make_async_copy(source(index), target(index), local_sems.at[stage, chunk])
        )
        for copy in copies:
            copy.start()
        return copies

    def arrived(copies):
        for copy in copies[:-1]:
            copy.wait_recv()
        copies[-1].wait()

    def lanes(index):
        return pl.ds(pl.multiple_of(index * LANES, LANES), LANES)

    def band_rows(index):
        return pl.ds(pl.multiple_of(index * span_x, span_x), span_x)

    started = []
    first, second, third, fourth = [], [], [], []
    for h in range(chunks):
        part = pl.ds(h * lines, lines)
        first.append(
            exchange(
                0,
                h,
                "py",
                lambda peer: spectrum_ref.at[peer, :, part],
                lambda index: columns_in.at[h, :, :, lanes(index)],
            )
        )
    for h in range(chunks):
        arrived(first[h])
        values = columns_in[h].reshape(rows_dev * lines, cols_dev * LANES)
        mixed = product(halves(values), (mix_upper[...], mix_lower[...]))
        for r in range(rows_dev):
            for j in range(step):
                start = r * lines + j * bands
                for p in range(packed):
                    rows_out[h, r, j, p * bands : (p + 1) * bands, :] = mixed[
                        start : start + bands, p * K : (p + 1) * K
                    ]
        second.append(
            exchange(
                1,
                h,
                "px",
                lambda peer: rows_out.at[h, peer],
                lambda index: rows_in.at[h, :, band_rows(index)],
            )
        )
    for h in range(chunks):
        arrived(second[h])
        wave = (wave_upper[...], wave_lower[...])
        for j in range(step):
            mixed = product(wave, halves(rows_in[h, j])) * gain_ref[h * step + j]
            back_out[h, j] = product(wave, halves(mixed))
        third.append(
            exchange(
                2,
                h,
                "px",
                lambda peer: back_out.at[h, :, band_rows(peer)],
                lambda index: back_in.at[h, index],
            )
        )
    for h in range(chunks):
        arrived(third[h])
        values = jnp.concatenate(
            [
                jnp.concatenate(
                    [back_in[h, r, j, p * bands : (p + 1) * bands, :] for p in range(packed)],
                    axis=1,
                )
                for r in range(rows_dev)
                for j in range(step)
            ],
            axis=0,
        )
        mixed = product(halves(values), (mix_upper[...], mix_lower[...]), transposed=True)
        columns_out[h] = mixed.reshape(rows_dev, lines, cols_dev * LANES)
        part = pl.ds(h * lines, lines)
        fourth.append(
            exchange(
                3,
                h,
                "py",
                lambda peer: columns_out.at[h, :, :, lanes(peer)],
                lambda index: out_ref.at[index, :, part],
            )
        )
    for h in range(chunks):
        arrived(fourth[h])
    for stage in (first, second, third, fourth):
        for copies in stage:
            for copy in copies[:-1]:
                copy.wait_send()


def convolve(spectrum, gain, mixing, matrix, bands):
    cols_dev, rows_dev, held, _ = spectrum.shape
    slab = held // bands
    chunks = 4
    while slab % chunks or (slab // chunks * bands) % 8:
        chunks //= 2
    step = slab // chunks
    lines = step * bands
    span_x = K // rows_dev
    peers = max(rows_dev, cols_dev)
    mix_upper, mix_lower = exact_halves(mixing)
    wave_upper, wave_lower = exact_halves(matrix)
    columns_shape = (chunks, rows_dev, lines, cols_dev * LANES)
    rows_shape = (chunks, rows_dev, step, span_x, K)
    full_shape = (chunks, step, K, K)

    def body(*refs):
        convolve_kernel((chunks, step, bands), *refs)

    whole = pl.BlockSpec(memory_space=pltpu.VMEM)
    return pl.pallas_call(
        body,
        out_shape=jax.ShapeDtypeStruct(spectrum.shape, jnp.float32),
        in_specs=[whole] * 6,
        out_specs=whole,
        scratch_shapes=[
            pltpu.VMEM(columns_shape, jnp.float32),
            pltpu.VMEM(rows_shape, jnp.float32),
            pltpu.VMEM(full_shape, jnp.float32),
            pltpu.VMEM(full_shape, jnp.float32),
            pltpu.VMEM(rows_shape, jnp.float32),
            pltpu.VMEM(columns_shape, jnp.float32),
            pltpu.SemaphoreType.DMA((4, chunks, peers)),
            pltpu.SemaphoreType.DMA((4, chunks, peers)),
            pltpu.SemaphoreType.DMA((4, chunks)),
        ],
        compiler_params=pltpu.CompilerParams(
            collective_id=0, has_side_effects=True, vmem_limit_bytes=56 * 2**20
        ),
        name="convolve",
    )(
        spectrum,
        gain,
        jnp.asarray(mix_upper),
        jnp.asarray(mix_lower),
        jnp.asarray(wave_upper),
        jnp.asarray(wave_lower),
    )


def transformed(grid, span_x, span_y, rows_dev, cols_dev):
    table = hartley()
    matrix = jnp.asarray(table)
    packed = LANES // span_y
    bands = span_x // packed
    span_z = K // cols_dev
    slab = span_z // rows_dev
    mixing = np.einsum("syk,pq->spyqk", table.reshape(cols_dev, span_y, K), np.eye(packed))
    mixing = mixing.reshape(cols_dev * LANES, packed * K).astype(np.float32)

    squared, profile = (jnp.asarray(values) for values in wave_profile())
    first = lax.axis_index("py") * span_z + lax.axis_index("px") * slab
    squared_z = lax.dynamic_slice(squared, (first,), (slab,))
    profile_z = lax.dynamic_slice(profile, (first,), (slab,))
    total = squared_z[:, None, None] + squared[None, :, None] + squared[None, None, :]
    gain = profile_z[:, None, None] * profile[None, :, None] * profile[None, None, :]
    gain = jnp.where(
        total > 0, (EWALD_GAIN / float(K**3)) * gain / jnp.where(total > 0, total, 1.0), 0.0
    )

    ordered = grid.reshape(packed, bands, span_y, K).transpose(1, 0, 2, 3).reshape(-1, K)
    spectrum = lax.dot_general(matrix, ordered, (((1,), (1,)), ((), ())), precision=HIGH)
    spectrum = spectrum.reshape(cols_dev, rows_dev, slab * bands, LANES)
    spectrum = convolve(spectrum, gain, mixing, table, bands)
    spectrum = spectrum.reshape(K, span_x * span_y)
    ordered = lax.dot_general(spectrum, matrix, (((0,), (0,)), ((), ())), precision=HIGH)
    return ordered.reshape(bands, packed, span_y, K).transpose(1, 0, 2, 3)


def per_device(fractions, charge, cell_index, destination, live_blocks):
    rows_dev = lax.axis_size("px")
    cols_dev = lax.axis_size("py")
    span_x = K // rows_dev
    span_y = K // cols_dev
    blocks, width = charge.shape
    capacity = max(2, 3 * blocks // (2 * cols_dev))
    slots = cols_dev * capacity
    padded = -(-slots // SORT_BLOCKS) * SORT_BLOCKS
    groups = padded // GROUP_BLOCKS
    rows = -(-(span_x + 5) // ROWS_CHUNK) * ROWS_CHUNK
    columns = -(-(span_y + 5) // 8) * 8

    alive = (jnp.arange(blocks, dtype=jnp.int32) < live_blocks[0]).astype(jnp.int32)
    target = destination[:, 0]
    matches = (target[:, None] == jnp.arange(cols_dev, dtype=jnp.int32)[None, :]).astype(jnp.int32)
    matches = matches * alive[:, None]
    earlier = jnp.cumsum(matches, axis=0) - matches
    position = jnp.sum(earlier * matches, axis=1)
    slot_of = jnp.where(alive > 0, target * capacity + position, -1)
    picked = (slot_of[None, :] == jnp.arange(slots, dtype=jnp.int32)[:, None]).astype(jnp.float32)
    payload = jnp.stack(
        [
            fractions[:, 0],
            fractions[:, 1],
            fractions[:, 2],
            charge,
            (cell_index // (span_y * K)).astype(jnp.float32),
            (cell_index // K % span_y).astype(jnp.float32),
            (cell_index % K).astype(jnp.float32),
            jnp.ones(charge.shape, jnp.float32),
        ],
        axis=1,
    )
    outgoing = jnp.dot(picked, payload.reshape(blocks, -1), precision=HIGHEST)
    outgoing = outgoing.reshape(cols_dev, capacity, 8, width)
    arrived = lax.all_to_all(outgoing, "py", split_axis=0, concat_axis=0, tiled=True)
    arrived = arrived.reshape(slots, 8, width)
    used = (arrived[:, 7, 0] > 0.5).astype(jnp.int32)
    place = jnp.where(used > 0, jnp.cumsum(used) - used, -1)
    chosen = (place[None, :] == jnp.arange(padded, dtype=jnp.int32)[:, None]).astype(jnp.float32)
    atoms = jnp.dot(chosen, arrived.reshape(slots, -1), precision=HIGHEST)
    batches = padded // SORT_BLOCKS
    members = SORT_BLOCKS * width
    atoms = (
        atoms.reshape(batches, SORT_BLOCKS, 8, width)
        .transpose(0, 2, 1, 3)
        .reshape(batches, 8, members)
    )
    number = jnp.arange(members, dtype=jnp.int32)
    key = jnp.where(atoms[:, 7] > 0.5, atoms[:, 4].astype(jnp.int32), K) * members + number
    rank = jnp.sum((key[:, None, :] < key[:, :, None]).astype(jnp.int32), axis=2)
    order = (rank[:, :, None] == number[None, None, :]).astype(jnp.float32)
    atoms = jnp.einsum("bcs,bsd->bcd", atoms, order, precision=HIGHEST)
    atoms = (
        atoms.reshape(batches, 8, members // (GROUP_BLOCKS * width), GROUP_BLOCKS * width)
        .transpose(0, 2, 1, 3)
        .reshape(groups, 8, GROUP_BLOCKS * width)
    )
    real = atoms[:, 7] > 0.5
    count = jnp.stack(
        [
            jnp.min(jnp.where(real, atoms[:, 4], 2.0 * K), axis=1),
            jnp.max(jnp.where(real, atoms[:, 4], -1.0 * K), axis=1),
        ]
    ).astype(jnp.int32)

    extended = deposit(count, atoms, rows, columns)
    moved_rows = from_behind(extended[span_x : span_x + 5], "px", 1)
    extended = jnp.concatenate([extended[:5] + moved_rows, extended[5:span_x]], axis=0)
    moved_cols = from_behind(extended[:, span_y : span_y + 5], "py", 1)
    grid = jnp.concatenate([extended[:, :5] + moved_cols, extended[:, 5:span_y]], axis=1)

    potential = transformed(
        grid.reshape(span_x * span_y, K), span_x, span_y, rows_dev, cols_dev
    ).reshape(span_x, span_y, K)
    lower_rows = from_behind(potential[:5], "px", -1)
    potential = jnp.concatenate([potential, lower_rows], axis=0)
    lower_cols = from_behind(potential[:, :5], "py", -1)
    potential = jnp.concatenate([potential, lower_cols], axis=1)
    potential = jnp.pad(
        potential, ((0, rows - span_x - 5), (0, columns - span_y - 5), (0, 0))
    )

    forces = pull(count, atoms, potential)[:, :3]
    forces = forces.reshape(batches, groups // batches, 3, -1).transpose(0, 2, 1, 3)
    forces = forces.reshape(batches, 3, members)
    forces = jnp.einsum("bcd,bsd->bcs", forces, order, precision=HIGHEST)
    forces = (
        forces.reshape(batches, 3, SORT_BLOCKS, width)
        .transpose(0, 2, 1, 3)
        .reshape(padded, 3 * width)
    )
    forces = lax.dot_general(chosen, forces, (((0,), (0,)), ((), ())), precision=HIGHEST)
    returned = lax.all_to_all(
        forces.reshape(cols_dev, capacity, 3, width), "py", split_axis=0, concat_axis=0, tiled=True
    ).reshape(slots, 3 * width)
    result = lax.dot_general(picked, returned, (((0,), (0,)), ((), ())), precision=HIGHEST)
    return result.reshape(blocks, 3, width)


def solution(mesh):
    split = (
        P(("px", "py"), None, None),
        P(("px", "py"), None),
        P(("px", "py"), None),
        P(("px", "py"), None),
        P(("px", "py")),
    )
    return jax.shard_map(
        per_device,
        mesh=mesh,
        in_specs=split,
        out_specs=P(("px", "py"), None, None),
        check_vma=False,
    )
```

profile of v0, /device:TPU:0, one launch (start us, length us, event | category | flops | bytes accessed | tf_op | source)
XLA Modules:
  0.0 289.9 jit_solution(2582906273426204917)
XLA Ops:
  0.7 0.7 fusion.36
  1.5 0.8 fusion.24
  2.3 0.8 constant_dynamic-update-slice_fusion.1
  3.1 0.7 bitcast_dynamic-update-slice_fusion
  3.8 0.7 fusion.28
  4.6 0.7 fusion.32
  5.3 0.7 fusion.35
  6.0 0.7 compare_select_fusion.4
  6.7 0.3 fusion.8
  7.0 0.7 copy.59
  7.7 5.2 %all-to-all-start = ((f32[8,6,8,128]{3,2,1,0:T(8,128)}), f32[8,6,8,128]{3,2,1,0:T(8,128)S(1)}, u32[]{:S(2)}, u32[]{:S(2)}) async-start(f32[8,6,8,128]{3,2,1,0:T(8,128)} %copy.59), calls=%async_computation | async-start | bytes 393216 | tf_op jit(solution)/shard_map/all_to_all | solution.py:509
  12.9 0.8 dynamic_slice.6
  13.6 0.8 dynamic_slice.7
  14.4 4.7 %all-to-all-done = f32[8,6,8,128]{3,2,1,0:T(8,128)S(1)} async-done(((f32[8,6,8,128]{3,2,1,0:T(8,128)}), f32[8,6,8,128]{3,2,1,0:T(8,128)S(1)}, u32[]{:S(2)}, u32[]{:S(2)}) %all-to-all-start) | async-done | bytes 196640 | tf_op jit(solution)/shard_map/all_to_all | solution.py:509
  19.1 0.9 fusion.48
  20.3 0.3 convolution_bitcast_fusion.1
  20.7 3.4 %convert_reduce_fusion = s32[6,1024]{1,0:T(8,128)S(1)} fusion(s32[6,1024]{1,0:T(8,128)S(1)} %bitcast_add_fusion, s32[6,1024]{1,0:T(8,128)S(1)} %bitcast.153), kind=kLoop, calls=%fused_computation.3 | loop fusion | flops 18868224 | bytes 73728 | tf_op jit(solution)/shard_map/reduce_sum | solution.py:524
  24.1 8.8 %fusion.1 = f32[6,8,1024]{2,1,0:T(8,128)S(1)} fusion(f32[6,8,1024]{2,1,0:T(8,128)S(1)} %reshape.280, s32[6,1024]{1,0:T(8,128)S(1)} %convert_reduce_fusion), kind=kOutput, calls=%fused_computation.2 | convolution fusion | flops 610271232 | bytes 417792 | tf_op jit(solution)/shard_map/bcs,bsd->bcd/dot_general | solution.py:526
  32.9 0.3 fusion.16
  33.2 30.7 %deposit.1 = f32[70,40,256]{2,1,0:T(8,128)S(1)} custom-call(s32[2,24]{1,0:T(2,128)S(1)} %maximum_convert_fusion.span_ref, f32[24,8,256]{2,1,0:T(8,128)S(1)} %bitcast.141), custom_call_target="tpu_custom_call" | custom-call | tf_op jit(solution)/shard_map/deposit/pallas_call | solution.py:191
  64.0 3.3 %collective-permute-start = (f32[5,40,256]{2,1,0:T(8,128)S(1)}, f32[5,40,256]{2,1,0:T(8,128)S(1)}, u32[]{:S(2)}, u32[]{:S(2)}) collective-permute-start(f32[5,40,256]{2,1,0:T(8,128)S(1)} %slice.87), channel_id=1, source_target_pairs={{0,8},{8,16},{16,24},{24,0},{1,9},{9,17},{17,25},{25,1},{2,10},{10... | collective-permute-start | bytes 614408 | tf_op jit(solution)/shard_map/ppermute | solution.py:42
  67.4 0.2 slice.88
  67.5 4.1 %collective-permute-done = f32[5,40,256]{2,1,0:T(8,128)S(1)} collective-permute-done((f32[5,40,256]{2,1,0:T(8,128)S(1)}, f32[5,40,256]{2,1,0:T(8,128)S(1)}, u32[]{:S(2)}, u32[]{:S(2)}) %collective-permute-start) | collective-permute-done | bytes 204832 | tf_op jit(solution)/shard_map/ppermute | solution.py:42
  71.7 0.2 collective-permute-start.1
  71.9 1.7 fusion.4.refs_1_
  73.7 7.8 %collective-permute-done.1 = f32[64,5,256]{2,1,0:T(8,128)S(1)} collective-permute-done((f32[64,5,256]{2,1,0:T(8,128)S(1)}, f32[64,5,256]{2,1,0:T(8,128)S(1)}, u32[]{:S(2)}, u32[]{:S(2)}) %collective-permute-start.1) | collective-permute-done | bytes 327712 | tf_op jit(solution)/shard_map/ppermute | solution.py:42
  81.4 0.1 maximum_add_fusion
  81.5 0.3 fusion.6
  81.9 0.1 copy.63
  82.0 0.8 copy-done.1
  82.8 1.2 fusion.50
  84.0 1.5 reshape.283.refs_0_
  85.5 113.9 %convolve.1 = f32[8,4,128,128]{3,2,1,0:T(8,128)} custom-call(f32[8,4,128,128]{3,2,1,0:T(8,128)} %reshape.283.refs_0_, f32[8,256,256]{2,1,0:T(8,128)} %fusion.4.refs_1_, bf16[1024,1024]{1,0:T(8,128)(2,1)} %constant.114.clone.refs_2_, bf16[1024,1024]{1,0:T(8,128)(2,1)} %constant.115.clone.refs_3_, bf16[256,256]{1,0:T(8,128)(2,1)} %constant.116.clone.refs_4_, ...), custom_call_target="tpu_custom_call" | custom-call | tf_op jit(solution)/shard_map/convolve/pallas_call | solution.py:414
  199.3 2.7 reshape.284
  202.0 2.0 copy.64
  204.0 1.0 convolution_bitcast_fusion
  205.0 0.2 copy.65
  205.3 6.9 %collective-permute-start.2 = (f32[5,32,256]{2,1,0:T(8,128)S(1)}, f32[5,32,256]{2,1,0:T(8,128)S(1)}, u32[]{:S(2)}, u32[]{:S(2)}) collective-permute-start(f32[5,32,256]{2,1,0:T(8,128)S(1)} %slice.89), channel_id=1, source_target_pairs={{0,24},{8,0},{16,8},{24,16},{1,25},{9,1},{17,9},{25,17},{2,26},{10... | collective-permute-start | bytes 491528 | tf_op jit(solution)/shard_map/ppermute | solution.py:42
  212.2 4.4 %collective-permute-done.2 = f32[5,32,256]{2,1,0:T(8,128)S(1)} collective-permute-done((f32[5,32,256]{2,1,0:T(8,128)S(1)}, f32[5,32,256]{2,1,0:T(8,128)S(1)}, u32[]{:S(2)}, u32[]{:S(2)}) %collective-permute-start.2) | collective-permute-done | bytes 163872 | tf_op jit(solution)/shard_map/ppermute | solution.py:42
  216.8 1.3 collective-permute-start.3
  218.3 4.8 %collective-permute-done.3 = f32[69,5,256]{2,0,1:T(8,128)S(1)} collective-permute-done((f32[69,5,256]{2,0,1:T(8,128)S(1)}, f32[69,5,256]{2,0,1:T(8,128)S(1)}, u32[]{:S(2)}, u32[]{:S(2)}) %collective-permute-start.3) | collective-permute-done | bytes 353312 | tf_op jit(solution)/shard_map/ppermute | solution.py:42
  223.1 0.1 copy.67
  223.2 0.2 select_maximum_fusion.potential_ref
  223.5 45.5 %pull.1 = f32[24,8,256]{2,1,0:T(8,128)S(1)} custom-call(s32[2,24]{1,0:T(2,128)S(1)} %maximum_convert_fusion.span_ref, f32[24,8,256]{2,1,0:T(8,128)S(1)} %bitcast.142, f32[70,40,256]{2,1,0:T(8,128)S(1)} %select_maximum_fusion.potential_ref), custom_call_target="tpu_custom_call" | custom-call | tf_op jit(solution)/shard_map/pull/pallas_call | solution.py:208
  269.0 12.1 %fusion = f32[6,3,1024]{2,1,0:T(4,128)S(1)} fusion(f32[6,3,1024]{2,1,0:T(4,128)S(1)} %bitcast.154, s32[6,1024]{1,0:T(8,128)S(1)} %convert_reduce_fusion), kind=kOutput, calls=%fused_computation.1 | convolution fusion | flops 232783872 | bytes 172032 | tf_op jit(solution)/shard_map/bcd,bsd->bcs/dot_general | solution.py:560
  281.2 0.2 fusion.13
  281.5 7.6 %all_to_all.10 = f32[8,6,3,128]{3,2,1,0:T(4,128)S(1)} all-to-all(f32[8,6,3,128]{3,2,1,0:T(4,128)S(1)} %copy.69), channel_id=1, replica_groups=mesh['px'=4,'py'=8] {'py'}, dimensions={0} | all-to-all | bytes 147456 | tf_op jit(solution)/shard_map/all_to_all | solution.py:567
  289.1 0.8 fusion.10
  (36 shorter events, 1.1 us)
Async XLA Ops:
  7.7 11.4 %all-to-all-start = ((f32[8,6,8,128]{3,2,1,0:T(8,128)}), f32[8,6,8,128]{3,2,1,0:T(8,128)S(1)}, u32[]{:S(2)}, u32[]{:S(2)}) async-start(f32[8,6,8,128]{3,2,1,0:T(8,128)} %copy.59), calls=%async_computation | async-start | bytes 393216 | tf_op jit(solution)/shard_map/all_to_all | solution.py:509
  32.9 34.4 %copy-start.2 = (f32[256]{0:T(256)S(1)}, f32[256]{0:T(256)}, u32[]{:S(2)}) copy-start(f32[256]{0:T(256)} %constant.112.clone) | copy-start | bytes 3076
  32.9 34.4 %copy-start.3 = (f32[256]{0:T(256)S(1)}, f32[256]{0:T(256)}, u32[]{:S(2)}) copy-start(f32[256]{0:T(256)} %constant.113.clone) | copy-start | bytes 3076
  64.0 7.6 %collective-permute-start = (f32[5,40,256]{2,1,0:T(8,128)S(1)}, f32[5,40,256]{2,1,0:T(8,128)S(1)}, u32[]{:S(2)}, u32[]{:S(2)}) collective-permute-start(f32[5,40,256]{2,1,0:T(8,128)S(1)} %slice.87), channel_id=1, source_target_pairs={{0,8},{8,16},{16,24},{24,0},{1,9},{9,17},{17,25},{25,1},{2,10},{10... | collective-permute-start | bytes 614408 | tf_op jit(solution)/shard_map/ppermute | solution.py:42
  71.7 9.7 %collective-permute-start.1 = (f32[64,5,256]{2,1,0:T(8,128)S(1)}, f32[64,5,256]{2,1,0:T(8,128)S(1)}, u32[]{:S(2)}, u32[]{:S(2)}) collective-permute-start(f32[64,5,256]{2,1,0:T(8,128)S(1)} %pad_maximum_fusion.1), channel_id=1, source_target_pairs={{0,1},{1,2},{2,3},{3,4},{4,5},{5,6},{6,7},{7,0},{8,9},{9,10},{10,1... | collective-permute-start | bytes 983048 | tf_op jit(solution)/shard_map/ppermute | solution.py:42
  81.9 1.0 copy-start.1
  202.0 2.0 copy-start
  205.3 11.3 %collective-permute-start.2 = (f32[5,32,256]{2,1,0:T(8,128)S(1)}, f32[5,32,256]{2,1,0:T(8,128)S(1)}, u32[]{:S(2)}, u32[]{:S(2)}) collective-permute-start(f32[5,32,256]{2,1,0:T(8,128)S(1)} %slice.89), channel_id=1, source_target_pairs={{0,24},{8,0},{16,8},{24,16},{1,25},{9,1},{17,9},{25,17},{2,26},{10... | collective-permute-start | bytes 491528 | tf_op jit(solution)/shard_map/ppermute | solution.py:42
  216.8 6.3 %collective-permute-start.3 = (f32[69,5,256]{2,0,1:T(8,128)S(1)}, f32[69,5,256]{2,0,1:T(8,128)S(1)}, u32[]{:S(2)}, u32[]{:S(2)}) collective-permute-start(f32[69,5,256]{2,0,1:T(8,128)S(1)} %copy.66), channel_id=1, source_target_pairs={{0,7},{1,0},{2,1},{3,2},{4,3},{5,4},{6,5},{7,6},{8,15},{9,8},{10,9... | collective-permute-start | bytes 1059848 | tf_op jit(solution)/shard_map/ppermute | solution.py:42
where the time goes:
time: 285 us; the launch traced here: 290 us
  Pallas kernels  190 us (67%)
  waiting for transfers between devices  25.7 us (9%)
  matrix products  24.7 us (9%)
  starting transfers between devices  16.9 us (6%)
  other arithmetic  12 us (4%)
  local copies, waits for them, and re-layouts  11.9 us (4%)
  blocking collectives  7.58 us (3%)
    pallas_call x1, Pallas kernels, convolve(): pl.pallas_call(body, out_shape=jax.ShapeDtypeStruct(spectrum.shape, jnp.f...  114 us
    pallas_call x1, Pallas kernels, pull(): pl.pallas_call(pull_kernel, out_shape=jax.ShapeDtypeStruct((groups, lines...  45.5 us
    pallas_call x1, Pallas kernels, deposit(): pl.pallas_call(deposit_kernel, out_shape=jax.ShapeDtypeStruct((rows, colu...  30.7 us
    ppermute x4, waiting for transfers between devices, from_behind(): return lax.ppermute(value, axis, pairs)  21 us
    dot_general x1, matrix products, per_device(): forces = jnp.einsum('bcd,bsd->bcs', forces, order, precision=HIGHEST)  12.1 us
    ppermute x4, starting transfers between devices, from_behind(): return lax.ppermute(value, axis, pairs)  11.7 us
    dot_general x1, matrix products, per_device(): atoms = jnp.einsum('bcs,bsd->bcd', atoms, order, precision=HIGHEST)  8.8 us
    all_to_all x1, blocking collectives, per_device(): lax.all_to_all(forces.reshape(cols_dev, capacity, 3, width), 'py', split_...  7.58 us
  transfers between devices with their start and end apart: 5, of which 5 were waited for; matrix products, arithmetic and copies ran while one was open for 1% of the time, Pallas kernels for 0%

commit v1 on v0

--- a/solution.py
+++ b/solution.py
@@ -470,6 +470,19 @@
     return ordered.reshape(bands, packed, span_y, K).transpose(1, 0, 2, 3)
 
 
+def permuted(form, values, order):
+    parts = []
+    for _ in range(3):
+        part = lax.reduce_precision(values, exponent_bits=8, mantissa_bits=7)
+        parts.append(part.astype(jnp.bfloat16))
+        values = values - part
+    moved = jnp.einsum(
+        form, jnp.concatenate(parts, axis=1), order, preferred_element_type=jnp.float32
+    )
+    upper, middle, lower = jnp.split(moved, 3, axis=1)
+    return (upper + middle) + lower
+
+
 def per_device(fractions, charge, cell_index, destination, live_blocks):
     rows_dev = lax.axis_size("px")
     cols_dev = lax.axis_size("py")
@@ -522,8 +535,8 @@
     number = jnp.arange(members, dtype=jnp.int32)
     key = jnp.where(atoms[:, 7] > 0.5, atoms[:, 4].astype(jnp.int32), K) * members + number
     rank = jnp.sum((key[:, None, :] < key[:, :, None]).astype(jnp.int32), axis=2)
-    order = (rank[:, :, None] == number[None, None, :]).astype(jnp.float32)
-    atoms = jnp.einsum("bcs,bsd->bcd", atoms, order, precision=HIGHEST)
+    order = (rank[:, :, None] == number[None, None, :]).astype(jnp.bfloat16)
+    atoms = permuted("bcs,bsd->bcd", atoms, order)
     atoms = (
         atoms.reshape(batches, 8, members // (GROUP_BLOCKS * width), GROUP_BLOCKS * width)
         .transpose(0, 2, 1, 3)
@@ -557,7 +570,7 @@
     forces = pull(count, atoms, potential)[:, :3]
     forces = forces.reshape(batches, groups // batches, 3, -1).transpose(0, 2, 1, 3)
     forces = forces.reshape(batches, 3, members)
-    forces = jnp.einsum("bcd,bsd->bcs", forces, order, precision=HIGHEST)
+    forces = permuted("bcd,bsd->bcs", forces, order)
     forces = (
         forces.reshape(batches, 3, SORT_BLOCKS, width)
         .transpose(0, 2, 1, 3)

time: 285 us -> 270 us (0.947); the launches traced: 290 us -> 268 us
  matrix products: 24.7 us -> 14.4 us
  Pallas kernels: 190 us -> 181 us
  starting transfers between devices: 16.9 us -> 12.8 us
    dot_general x2, matrix products: 20.9 us -> 10.7 us  [permuted(): jnp.einsum(form, jnp.concatenate(parts, axis=1), order, preferred_element...]
    pallas_call x1, Pallas kernels: 45.5 us -> 39.1 us  [pull(): pl.pallas_call(pull_kernel, out_shape=jax.ShapeDtypeStruct((groups, lines...]
    pallas_call x1, Pallas kernels: 30.7 us -> 26.4 us  [deposit(): pl.pallas_call(deposit_kernel, out_shape=jax.ShapeDtypeStruct((rows, colu...]
    ppermute x4, starting transfers between devices: 11.7 us -> 7.62 us  [from_behind(): return lax.ppermute(value, axis, pairs)]
where the time goes in v1:
time: 270 us; the launch traced here: 268 us
  Pallas kernels  181 us (67%)
  waiting for transfers between devices  27.5 us (10%)
  matrix products  14.4 us (5%)
  starting transfers between devices  12.8 us (5%)
  other arithmetic  12.2 us (5%)
  local copies, waits for them, and re-layouts  11.9 us (4%)
  blocking collectives  7.58 us (3%)
    pallas_call x1, Pallas kernels, convolve(): pl.pallas_call(body, out_shape=jax.ShapeDtypeStruct(spectrum.shape, jnp.f...  116 us
    pallas_call x1, Pallas kernels, pull(): pl.pallas_call(pull_kernel, out_shape=jax.ShapeDtypeStruct((groups, lines...  39.1 us
    pallas_call x1, Pallas kernels, deposit(): pl.pallas_call(deposit_kernel, out_shape=jax.ShapeDtypeStruct((rows, colu...  26.4 us
    ppermute x4, waiting for transfers between devices, from_behind(): return lax.ppermute(value, axis, pairs)  22.8 us
    dot_general x2, matrix products, permuted(): jnp.einsum(form, jnp.concatenate(parts, axis=1), order, preferred_element...  10.7 us
    ppermute x4, starting transfers between devices, from_behind(): return lax.ppermute(value, axis, pairs)  7.62 us
    all_to_all x1, blocking collectives, per_device(): lax.all_to_all(forces.reshape(cols_dev, capacity, 3, width), 'py', split_...  7.58 us
  transfers between devices with their start and end apart: 5, of which 5 were waited for; matrix products, arithmetic and copies ran while one was open for 1% of the time, Pallas kernels for 0%

profile of v1, /device:TPU:0, one launch (start us, length us, event | category | flops | bytes accessed | tf_op | source)
XLA Modules:
  0.0 268.4 jit_solution(14753046001017638461)
XLA Ops:
  0.7 0.7 fusion.50
  1.5 0.8 fusion.38
  2.3 0.8 constant_dynamic-update-slice_fusion.1
  3.1 0.7 bitcast_dynamic-update-slice_fusion
  3.8 0.7 fusion.42
  4.6 0.7 fusion.46
  5.3 0.7 fusion.49
  6.0 0.7 compare_select_fusion.4
  6.7 0.3 fusion.20
  7.0 0.7 copy.59
  7.7 5.2 %all-to-all-start = ((f32[8,6,8,128]{3,2,1,0:T(8,128)}), f32[8,6,8,128]{3,2,1,0:T(8,128)S(1)}, u32[]{:S(2)}, u32[]{:S(2)}) async-start(f32[8,6,8,128]{3,2,1,0:T(8,128)} %copy.59), calls=%async_computation | async-start | bytes 393216 | tf_op jit(solution)/shard_map/all_to_all | solution.py:522
  12.9 0.8 dynamic_slice.6
  13.6 0.8 dynamic_slice.7
  14.4 4.7 %all-to-all-done = f32[8,6,8,128]{3,2,1,0:T(8,128)S(1)} async-done(((f32[8,6,8,128]{3,2,1,0:T(8,128)}), f32[8,6,8,128]{3,2,1,0:T(8,128)S(1)}, u32[]{:S(2)}, u32[]{:S(2)}) %all-to-all-start) | async-done | bytes 196640 | tf_op jit(solution)/shard_map/all_to_all | solution.py:522
  19.1 0.9 fusion.64
  20.3 0.3 convolution_bitcast_fusion.1
  20.8 3.4 %convert_reduce_fusion = s32[6,1024]{1,0:T(8,128)S(1)} fusion(s32[6,1024]{1,0:T(8,128)S(1)} %bitcast_add_fusion, s32[6,1024]{1,0:T(8,128)S(1)} %bitcast.152), kind=kLoop, calls=%fused_computation.3 | loop fusion | flops 18868224 | bytes 73728 | tf_op jit(solution)/shard_map/reduce_sum | solution.py:537
  24.1 5.1 %fusion.1 = f32[6,24,1024]{2,1,0:T(8,128)S(1)} fusion(s32[6,1024]{1,0:T(8,128)S(1)} %convert_reduce_fusion, bf16[6,8,1024]{2,1,0:T(8,128)(2,1)S(1)} %get-tuple-element.16, bf16[6,8,1024]{2,1,0:T(8,128)(2,1)S(1)} %get-tuple-element.17, bf16[6,8,1024]{2,1,0:T(8,128)(2,1)S(1)} %get-tuple-element.15), kind=kOutput, calls=%fused_computation.2 | convolution fusion | flops 309166080 | bytes 909312 | tf_op jit(solution)/shard_map/bcs,bsd->bcd/dot_general | solution.py:479
  29.4 0.3 fusion.30
  29.7 26.4 %deposit.1 = f32[70,40,256]{2,1,0:T(8,128)S(1)} custom-call(s32[2,24]{1,0:T(2,128)S(1)} %maximum_convert_fusion.span_ref, f32[24,8,256]{2,1,0:T(8,128)S(1)} %bitcast.139), custom_call_target="tpu_custom_call" | custom-call | tf_op jit(solution)/shard_map/deposit/pallas_call | solution.py:191
  56.1 2.2 collective-permute-start
  58.4 0.2 slice.88
  58.6 5.8 %collective-permute-done = f32[5,40,256]{2,1,0:T(8,128)S(1)} collective-permute-done((f32[5,40,256]{2,1,0:T(8,128)S(1)}, f32[5,40,256]{2,1,0:T(8,128)S(1)}, u32[]{:S(2)}, u32[]{:S(2)}) %collective-permute-start) | collective-permute-done | bytes 204832 | tf_op jit(solution)/shard_map/ppermute | solution.py:42
  64.5 0.2 collective-permute-start.1
  64.8 1.7 fusion.4.refs_1_
  66.5 7.8 %collective-permute-done.1 = f32[64,5,256]{2,1,0:T(8,128)S(1)} collective-permute-done((f32[64,5,256]{2,1,0:T(8,128)S(1)}, f32[64,5,256]{2,1,0:T(8,128)S(1)}, u32[]{:S(2)}, u32[]{:S(2)}) %collective-permute-start.1) | collective-permute-done | bytes 327712 | tf_op jit(solution)/shard_map/ppermute | solution.py:42
  74.3 0.1 maximum_add_fusion
  74.4 0.3 fusion.6
  74.7 0.1 copy.63
  74.9 0.8 copy-done.1
  75.7 1.2 fusion.66
  76.8 1.5 reshape.283.refs_0_
  78.3 115.5 %convolve.1 = f32[8,4,128,128]{3,2,1,0:T(8,128)} custom-call(f32[8,4,128,128]{3,2,1,0:T(8,128)} %reshape.283.refs_0_, f32[8,256,256]{2,1,0:T(8,128)} %fusion.4.refs_1_, bf16[1024,1024]{1,0:T(8,128)(2,1)} %constant.114.clone.refs_2_, bf16[1024,1024]{1,0:T(8,128)(2,1)} %constant.115.clone.refs_3_, bf16[256,256]{1,0:T(8,128)(2,1)} %constant.116.clone.refs_4_, ...), custom_call_target="tpu_custom_call" | custom-call | tf_op jit(solution)/shard_map/convolve/pallas_call | solution.py:414
  193.8 2.7 %reshape.284 = f32[256,2048]{1,0:T(8,128)} reshape(f32[8,4,128,128]{3,2,1,0:T(8,128)} %convolve.1) | data formatting | bytes 4194304 | tf_op jit(solution)/shard_map/reshape | solution.py:468
  196.5 2.0 copy.64
  198.5 1.0 convolution_bitcast_fusion
  199.5 0.2 copy.65
  199.8 3.5 %collective-permute-start.2 = (f32[5,32,256]{2,1,0:T(8,128)S(1)}, f32[5,32,256]{2,1,0:T(8,128)S(1)}, u32[]{:S(2)}, u32[]{:S(2)}) collective-permute-start(f32[5,32,256]{2,1,0:T(8,128)S(1)} %slice.89), channel_id=1, source_target_pairs={{0,24},{8,0},{16,8},{24,16},{1,25},{9,1},{17,9},{25,17},{2,26},{10... | collective-permute-start | bytes 491528 | tf_op jit(solution)/shard_map/ppermute | solution.py:42
  203.2 4.4 %collective-permute-done.2 = f32[5,32,256]{2,1,0:T(8,128)S(1)} collective-permute-done((f32[5,32,256]{2,1,0:T(8,128)S(1)}, f32[5,32,256]{2,1,0:T(8,128)S(1)}, u32[]{:S(2)}, u32[]{:S(2)}) %collective-permute-start.2) | collective-permute-done | bytes 163872 | tf_op jit(solution)/shard_map/ppermute | solution.py:42
  207.8 1.7 collective-permute-start.3
  209.8 4.8 %collective-permute-done.3 = f32[69,5,256]{2,0,1:T(8,128)S(1)} collective-permute-done((f32[69,5,256]{2,0,1:T(8,128)S(1)}, f32[69,5,256]{2,0,1:T(8,128)S(1)}, u32[]{:S(2)}, u32[]{:S(2)}) %collective-permute-start.3) | collective-permute-done | bytes 353312 | tf_op jit(solution)/shard_map/ppermute | solution.py:42
  214.6 0.1 copy.67
  214.7 0.2 select_maximum_fusion.potential_ref
  215.0 39.1 %pull.1 = f32[24,8,256]{2,1,0:T(8,128)S(1)} custom-call(s32[2,24]{1,0:T(2,128)S(1)} %maximum_convert_fusion.span_ref, f32[24,8,256]{2,1,0:T(8,128)S(1)} %bitcast.140, f32[70,40,256]{2,1,0:T(8,128)S(1)} %select_maximum_fusion.potential_ref), custom_call_target="tpu_custom_call" | custom-call | tf_op jit(solution)/shard_map/pull/pallas_call | solution.py:208
  254.1 5.5 %fusion = f32[6,9,1024]{2,1,0:T(8,128)S(1)} fusion(s32[6,1024]{1,0:T(8,128)S(1)} %convert_reduce_fusion, bf16[6,3,1024]{2,1,0:T(4,128)(2,1)S(1)} %get-tuple-element.19, bf16[6,3,1024]{2,1,0:T(4,128)(2,1)S(1)} %get-tuple-element.20, bf16[6,3,1024]{2,1,0:T(4,128)(2,1)S(1)} %get-tuple-element.18), kind=kOutput, calls=%fused_computation.1 | convolution fusion | flops 119869440 | bytes 356352 | tf_op jit(solution)/shard_map/bcd,bsd->bcs/dot_general | solution.py:479
  259.8 0.2 fusion.27
  260.0 7.6 %all_to_all.10 = f32[8,6,3,128]{3,2,1,0:T(4,128)S(1)} all-to-all(f32[8,6,3,128]{3,2,1,0:T(4,128)S(1)} %copy.69), channel_id=1, replica_groups=mesh['px'=4,'py'=8] {'py'}, dimensions={0} | all-to-all | bytes 147456 | tf_op jit(solution)/shard_map/all_to_all | solution.py:580
  267.6 0.8 fusion.24
  (40 shorter events, 1.3 us)
Async XLA Ops:
  7.7 11.4 %all-to-all-start = ((f32[8,6,8,128]{3,2,1,0:T(8,128)}), f32[8,6,8,128]{3,2,1,0:T(8,128)S(1)}, u32[]{:S(2)}, u32[]{:S(2)}) async-start(f32[8,6,8,128]{3,2,1,0:T(8,128)} %copy.59), calls=%async_computation | async-start | bytes 393216 | tf_op jit(solution)/shard_map/all_to_all | solution.py:522
  29.3 29.1 %copy-start.2 = (f32[256]{0:T(256)S(1)}, f32[256]{0:T(256)}, u32[]{:S(2)}) copy-start(f32[256]{0:T(256)} %constant.112.clone) | copy-start | bytes 3076
  29.3 29.0 %copy-start.3 = (f32[256]{0:T(256)S(1)}, f32[256]{0:T(256)}, u32[]{:S(2)}) copy-start(f32[256]{0:T(256)} %constant.113.clone) | copy-start | bytes 3076
  56.1 8.3 %collective-permute-start = (f32[5,40,256]{2,1,0:T(8,128)S(1)}, f32[5,40,256]{2,1,0:T(8,128)S(1)}, u32[]{:S(2)}, u32[]{:S(2)}) collective-permute-start(f32[5,40,256]{2,1,0:T(8,128)S(1)} %slice.87), channel_id=1, source_target_pairs={{0,8},{8,16},{16,24},{24,0},{1,9},{9,17},{17,25},{25,1},{2,10},{10... | collective-permute-start | bytes 614408 | tf_op jit(solution)/shard_map/ppermute | solution.py:42
  64.5 9.7 %collective-permute-start.1 = (f32[64,5,256]{2,1,0:T(8,128)S(1)}, f32[64,5,256]{2,1,0:T(8,128)S(1)}, u32[]{:S(2)}, u32[]{:S(2)}) collective-permute-start(f32[64,5,256]{2,1,0:T(8,128)S(1)} %pad_maximum_fusion.1), channel_id=1, source_target_pairs={{0,1},{1,2},{2,3},{3,4},{4,5},{5,6},{6,7},{7,0},{8,9},{9,10},{10,1... | collective-permute-start | bytes 983048 | tf_op jit(solution)/shard_map/ppermute | solution.py:42
  74.7 1.0 copy-start.1
  196.5 2.0 copy-start
  199.8 7.9 %collective-permute-start.2 = (f32[5,32,256]{2,1,0:T(8,128)S(1)}, f32[5,32,256]{2,1,0:T(8,128)S(1)}, u32[]{:S(2)}, u32[]{:S(2)}) collective-permute-start(f32[5,32,256]{2,1,0:T(8,128)S(1)} %slice.89), channel_id=1, source_target_pairs={{0,24},{8,0},{16,8},{24,16},{1,25},{9,1},{17,9},{25,17},{2,26},{10... | collective-permute-start | bytes 491528 | tf_op jit(solution)/shard_map/ppermute | solution.py:42
  207.8 6.7 %collective-permute-start.3 = (f32[69,5,256]{2,0,1:T(8,128)S(1)}, f32[69,5,256]{2,0,1:T(8,128)S(1)}, u32[]{:S(2)}, u32[]{:S(2)}) collective-permute-start(f32[69,5,256]{2,0,1:T(8,128)S(1)} %copy.66), channel_id=1, source_target_pairs={{0,7},{1,0},{2,1},{3,2},{4,3},{5,4},{6,5},{7,6},{8,15},{9,8},{10,9... | collective-permute-start | bytes 1059848 | tf_op jit(solution)/shard_map/ppermute | solution.py:42
